TPU v7x, 32 devices: a whole 2x2x4 slice. The times are simulated.
32 devices in a mesh: groups: 2 (over x), node: 16 (over z, y, core).
Axes of the slice: x: 2, y: 2, z: 4, core: 2. Of those that a mesh axis runs over, the one named last changes fastest.
Arguments:
- node_latent: bfloat16 [6144, 512], P(('groups', 'node')), parts along dimension 0, may hold values from -6 to 6
- edge_latent: bfloat16 [49152, 512], P(('groups', 'node')), parts along dimension 0, may hold values from -6 to 6
- node_cotangent: bfloat16 [6144, 512], P(('groups', 'node')), parts along dimension 0, may hold values from -6 to 6
- edge_cotangent: bfloat16 [49152, 512], P(('groups', 'node')), parts along dimension 0, may hold values from -6 to 6
- sender_slot: int32 [49152], P(('groups', 'node')), parts along dimension 0, may hold values from 0 to 319, as said below
- receiver: int32 [49152], P(('groups', 'node')), parts along dimension 0, may hold values from 0 to 191
- send_index: int32 [32, 16, 8], P(('groups', 'node')), parts along dimension 0, may hold values from 0 to 192, as said below
- edge_w1: bfloat16 [1536, 512], replicated, may hold values from -0.15625 to 0.15625
- edge_w2: bfloat16 [512, 512], replicated, may hold values from -0.25 to 0.25
- edge_gain: float32 [512], replicated, may hold values from 0.1 to 1.9
- node_w1: bfloat16 [1024, 512], replicated, may hold values from -0.1875 to 0.1875
- node_w2: bfloat16 [512, 512], replicated, may hold values from -0.25 to 0.25
- node_gain: float32 [512], replicated, may hold values from 0.1 to 1.9
Outputs:
- node_grad: bfloat16 [6144, 512], P(('groups', 'node')), parts along dimension 0
- edge_grad: bfloat16 [49152, 512], P(('groups', 'node')), parts along dimension 0
- edge_w1_grad: float32 [3072, 512], P(('groups', 'node')), parts along dimension 0
- edge_w2_grad: float32 [1024, 512], P(('groups', 'node')), parts along dimension 0
- edge_gain_grad: float32 [1024], P(('groups', 'node')), parts along dimension 0
- node_w1_grad: float32 [2048, 512], P(('groups', 'node')), parts along dimension 0
- node_w2_grad: float32 [1024, 512], P(('groups', 'node')), parts along dimension 0
- node_gain_grad: float32 [1024], P(('groups', 'node')), parts along dimension 0
There are 2 independent parts, one for each index of `groups`. A program takes and returns all parts, laid end to end along the dimension named above; an argument that names none is the same for every part. Nothing has to cross between parts.
Inputs may be any that keep to these rules, and one draw needn't show every extreme that they name: send_index[d, p, c] is the index within device d's block of the node that d sends to device p in slot c, and 192 marks an empty slot; the filled slots of a pair come first, a device sends nothing to itself, and the pair from device 16 - 1 to device 0 fills all 8 slots. `sender_slot`: for an edge on device p, a value v below 192 names node v of p's block; a value 192 + d * 8 + c names slot c of what device d sends to p, which is always a filled slot, and every filled slot is named by some edge of p.
All inputs are finite; a program needn't handle non-finite values.
Results may differ from a plain program's by a relative error of at most 0.008.
Values may be sent and summed in bfloat16 or wider, within the bound.
A program may use at most 128 MiB of HBM per device.

v0:
```python
import math

import jax
import jax.numpy as jnp
from jax import lax
from jax.sharding import PartitionSpec as P


def normalize(values):
    mean = jnp.mean(values, axis=-1, keepdims=True)
    centred = values - mean
    inverse = lax.rsqrt(jnp.mean(centred * centred, axis=-1, keepdims=True) + 1e-05)
    return (centred * inverse, inverse)


def norm_back(grad, normed, inverse, gain):
    scaled = grad * gain
    first = jnp.mean(scaled, axis=-1, keepdims=True)
    second = jnp.mean(scaled * normed, axis=-1, keepdims=True)
    return inverse * (scaled - first - normed * second)


def silu_back(grad, pre):
    sig = jax.nn.sigmoid(pre)
    return grad * sig * (1.0 + pre * (1.0 - sig))


def contract_rows(left, right):
    return lax.dot_general(
        left, right, (((0,), (0,)), ((), ())), preferred_element_type=jnp.float32
    )


def contract_cols(left, right):
    return lax.dot_general(
        left, right, (((1,), (1,)), ((), ())), preferred_element_type=jnp.float32
    )


def local(
    node_latent,
    edge_latent,
    node_cotangent,
    edge_cotangent,
    sender_slot,
    receiver,
    send_index,
    edge_w1,
    edge_w2,
    edge_gain,
    node_w1,
    node_w2,
    node_gain,
):
    devices = lax.axis_size("node")
    nodes_here = node_latent.shape[0]
    edges_here = edge_latent.shape[0]
    width = node_latent.shape[1]
    capacity = send_index.shape[2]
    node_scale = 1.0 / math.sqrt(nodes_here * devices)
    edge_scale = 1.0 / math.sqrt(edges_here * devices)
    padded = jnp.concatenate([node_latent, jnp.zeros((1, width), jnp.bfloat16)], axis=0)
    outgoing = padded[send_index[0]]
    incoming = lax.all_to_all(outgoing, "node", split_axis=0, concat_axis=0, tiled=True)
    table = jnp.concatenate([node_latent, incoming.reshape(devices * capacity, width)], axis=0)
    sender_rows = table[sender_slot]
    incidence = (receiver[:, None] == jnp.arange(nodes_here, dtype=jnp.int32)[None, :]).astype(
        jnp.bfloat16
    )
    receiver_rows = jnp.dot(incidence, node_latent, preferred_element_type=jnp.float32).astype(
        jnp.bfloat16
    )
    edge_input = jnp.concatenate([edge_latent, sender_rows, receiver_rows], axis=1)
    edge_pre = jnp.dot(edge_input, edge_w1, preferred_element_type=jnp.float32)
    edge_hidden = (edge_pre * jax.nn.sigmoid(edge_pre)).astype(jnp.bfloat16)
    edge_out = jnp.dot(edge_hidden, edge_w2, preferred_element_type=jnp.float32)
    edge_hat, edge_inv = normalize(edge_out)
    updated = (edge_latent.astype(jnp.float32) + edge_hat * edge_gain).astype(jnp.bfloat16)
    aggregate = contract_rows(incidence, updated).astype(jnp.bfloat16)
    node_input = jnp.concatenate([node_latent, aggregate], axis=1)
    node_pre = jnp.dot(node_input, node_w1, preferred_element_type=jnp.float32)
    node_hidden = (node_pre * jax.nn.sigmoid(node_pre)).astype(jnp.bfloat16)
    node_out = jnp.dot(node_hidden, node_w2, preferred_element_type=jnp.float32)
    node_hat, node_inv = normalize(node_out)
    node_dy = node_cotangent.astype(jnp.float32)
    node_gain_part = jnp.sum(node_dy * node_hat, axis=0) * node_scale
    node_mgrad = norm_back(node_dy, node_hat, node_inv, node_gain).astype(jnp.bfloat16)
    node_w2_part = contract_rows(node_hidden, node_mgrad) * node_scale
    node_agrad = silu_back(contract_cols(node_mgrad, node_w2), node_pre).astype(jnp.bfloat16)
    node_w1_part = contract_rows(node_input, node_agrad) * node_scale
    node_xgrad = contract_cols(node_agrad, node_w1)
    edge_total = edge_cotangent.astype(jnp.float32) + node_xgrad[:, width:][receiver]
    edge_gain_part = jnp.sum(edge_total * edge_hat, axis=0) * edge_scale
    edge_mgrad = norm_back(edge_total, edge_hat, edge_inv, edge_gain).astype(jnp.bfloat16)
    edge_w2_part = contract_rows(edge_hidden, edge_mgrad) * edge_scale
    edge_agrad = silu_back(contract_cols(edge_mgrad, edge_w2), edge_pre).astype(jnp.bfloat16)
    edge_xgrad = contract_cols(edge_agrad, edge_w1)
    edge_grad = (edge_total + edge_xgrad[:, :width]).astype(jnp.bfloat16)
    slot_sums = jax.ops.segment_sum(
        edge_xgrad[:, width : 2 * width], sender_slot, num_segments=nodes_here + devices * capacity
    )
    target_sums = jax.ops.segment_sum(edge_xgrad[:, 2 * width :], receiver, num_segments=nodes_here)
    returned = lax.all_to_all(
        slot_sums[nodes_here:].reshape(devices, capacity, width).astype(jnp.bfloat16),
        "node",
        split_axis=0,
        concat_axis=0,
        tiled=True,
    ).astype(jnp.float32)
    remote_sums = jax.ops.segment_sum(
        returned.reshape(devices * capacity, width),
        send_index[0].reshape(devices * capacity),
        num_segments=nodes_here + 1,
    )[:nodes_here]
    node_grad = (
        node_dy + node_xgrad[:, :width] + target_sums + slot_sums[:nodes_here] + remote_sums
    ).astype(jnp.bfloat16)
    edge_w1_grad = lax.psum_scatter(
        contract_rows(edge_input, edge_agrad) * edge_scale, "node", scatter_dimension=0, tiled=True
    )
    edge_w2_grad, edge_gain_grad, node_w1_grad, node_w2_grad, node_gain_grad = (
        lax.psum_scatter(edge_w2_part, "node", scatter_dimension=0, tiled=True),
        lax.psum_scatter(edge_gain_part, "node", scatter_dimension=0, tiled=True),
        lax.psum_scatter(node_w1_part, "node", scatter_dimension=0, tiled=True),
        lax.psum_scatter(node_w2_part, "node", scatter_dimension=0, tiled=True),
        lax.psum_scatter(node_gain_part, "node", scatter_dimension=0, tiled=True),
    )
    return (
        node_grad,
        edge_grad,
        edge_w1_grad,
        edge_w2_grad,
        edge_gain_grad,
        node_w1_grad,
        node_w2_grad,
        node_gain_grad,
    )


def solution(mesh):
    placed = (
        P(("groups", "node"), None),
        P(("groups", "node"), None),
        P(("groups", "node"), None),
        P(("groups", "node"), None),
        P(("groups", "node")),
        P(("groups", "node")),
        P(("groups", "node"), None, None),
        P(),
        P(),
        P(),
        P(),
        P(),
        P(),
    )
    return jax.shard_map(
        local,
        mesh=mesh,
        in_specs=placed,
        out_specs=(
            P(("groups", "node"), None),
            P(("groups", "node"), None),
            P(("groups", "node"), None),
            P(("groups", "node"), None),
            P(("groups", "node")),
            P(("groups", "node"), None),
            P(("groups", "node"), None),
            P(("groups", "node")),
        ),
        check_vma=False,
    )
```

profile of v0, /device:TPU:0, one launch (start us, length us, event | category | flops | bytes accessed | tf_op | source)
XLA Modules:
  0.0 313.2 jit_solution(17013548993188278721)
XLA Ops:
  10.6 7.4 %all-to-all-start = ((bf16[16,8,512]{2,1,0:T(8,128)(2,1)}), bf16[16,8,512]{2,1,0:T(8,128)(2,1)S(1)}, u32[]{:S(2)}, u32[]{:S(2)}) async-start(bf16[16,8,512]{2,1,0:T(8,128)(2,1)} %bitcast.1), calls=%async_computation | async-start | bytes 262144 | tf_op jit(solution)/shard_map/all_to_all | solution.py:64
  20.1 2.6 copy.39
  28.0 5.4 %gather_fusion.1 = bf16[1536,512]{1,0:T(8,128)(2,1)} fusion(bf16[320,512]{1,0:T(8,128)(2,1)S(1)} %pad_maximum_fusion.4, s32[2048]{0:T(1024)S(1)} %pad_clamp_fusion.1), kind=kCustom, calls=%fused_computation.1 | custom fusion | bytes 3151872 | tf_op jit(solution)/shard_map/gather | solution.py:66
  33.5 2.6 copy.42
  36.1 7.1 %multiply_convert_fusion.1 = (bf16[1536,512]{1,0:T(8,128)(2,1)S(1)}, f32[1536,512]{1,0:T(8,128)}) fusion(bf16[1536,512]{1,0:T(8,128)(2,1)S(1)} %copy-done, bf16[1536,512]{0,1:T(8,128)(2,1)} %convolution_convert_fusion, bf16[1536,512]{0,1:T(8,128)(2,1)} %copy.42, bf16[1536,512]{0,1:T(8,128)(2,1)} %copy.39), kind=kOutput, calls=%fused_computation.21 | convolution fusion | flops 2434007040 | bytes 11010048 | tf_op jit(solution)/shard_map/dot_general | solution.py:74
  44.7 2.1 copy-done.14
  54.6 5.3 %gather_fusion.2 = f32[1536,512]{1,0:T(8,128)} fusion(f32[192,512]{1,0:T(8,128)S(1)} %slice.40, s32[2048]{0:T(1024)} %pad_clamp_fusion), kind=kCustom, calls=%fused_computation.2 | custom fusion | bytes 6297600 | tf_op jit(solution)/shard_map/gather | solution.py:92
  59.9 3.6 %copy.44 = f32[1536,512]{0,1:T(8,128)} copy(f32[1536,512]{1,0:T(8,128)} %gather_fusion.2) | data formatting | bytes 6291456 | tf_op jit(solution)/shard_map/gather | solution.py:92
  63.5 4.8 %multiply_reduce_fusion = (f32[512]{0:T(512)}, f32[1536]{0:T(1024)S(1)}, f32[1536]{0:T(1024)S(1)}) fusion(f32[1536,512]{0,1:T(8,128)} %copy-done.1, f32[1536]{0:T(1024)S(1)} %add_rsqrt_fusion, f32[1536]{0:T(1024)S(1)} %broadcast_multiply_fusion.2, f32[1536,512]{0,1:T(8,128)} %copy.44, bf16[1536,512]{0,1:T(8,128)(2,1)S(1)} %copy.43, f32[512]{0:T(512)S(1)} %copy-done.30), kind=kLoop, calls=%fused_computation.14 | loop fusion | flops 7860736 | bytes 7892992 | tf_op jit(solution)/shard_map/reduce_sum | solution.py:93
  70.8 2.1 convolution_multiply_fusion.3
  72.9 2.8 convolution_multiply_fusion.2
  75.8 4.5 %fusion.5 = bf16[1536,512]{1,0:T(8,128)(2,1)S(1)} fusion(f32[1536,512]{1,0:T(8,128)} %get-tuple-element.41, bf16[1536,512]{0,1:T(8,128)(2,1)} %copy-done.18, bf16[512,512]{1,0:T(8,128)(2,1)} %param.21), kind=kOutput, calls=%fused_computation.23 | convolution fusion | flops 812384256 | bytes 6815744 | tf_op jit(solution)/shard_map/dot_general | solution.py:35
  81.5 6.3 %convolution_multiply_fusion = f32[1536,512]{1,0:T(8,128)} fusion(bf16[1536,512]{1,0:T(8,128)(2,1)S(1)} %fusion.5, bf16[1536,512]{0,1:T(8,128)(2,1)S(1)} %copy-done.16, bf16[1536,512]{0,1:T(8,128)(2,1)S(1)} %copy-done.17, bf16[1536,512]{0,1:T(8,128)(2,1)S(1)} %copy-done.15), kind=kOutput, calls=%fused_computation.7 | convolution fusion | flops 2430861312 | bytes 9437184 | tf_op jit(solution)/shard_map/dot_general | solution.py:29
  90.4 4.1 %fusion.45 = f32[1536,1536]{1,0:T(8,128)S(1)} fusion(bf16[1536,512]{1,0:T(8,128)(2,1)} %copy-done.34, bf16[1536,512]{1,0:T(8,128)(2,1)S(1)} %copy-done), kind=kOutput, calls=%fused_computation.94 | convolution fusion | flops 2415919104 | bytes 12582912 | tf_op jit(solution)/shard_map/dot_general | solution.py:35
  94.5 3.6 %copy-done.4 = f32[1536,1536]{1,0:T(8,128)} copy-done((f32[1536,1536]{1,0:T(8,128)}, f32[1536,1536]{1,0:T(8,128)S(1)}, u32[]{:S(2)}) %copy-start.4) | copy-done | bytes 9437208
  100.1 11.3 %scatter_custom_fusion = f32[320,512]{1,0:T(8,128)} fusion(s32[1536]{0:T(1024)} %param.17, f32[1536,1536]{1,0:T(8,128)} %copy-done.4, f32[]{:T(128)} %constant.16.clone.1), kind=kCustom, calls=%fused_computation.12 | custom fusion | flops 786432 | bytes 3801600 | tf_op jit(solution)/shard_map/scatter-add | solution.py:99
  113.0 6.1 %all-to-all-start.1 = ((bf16[16,8,512]{2,1,0:T(8,128)(2,1)}), bf16[16,8,512]{2,1,0:T(8,128)(2,1)}, u32[]{:S(2)}, u32[]{:S(2)}) async-start(bf16[16,8,512]{2,1,0:T(8,128)(2,1)} %fusion.33), calls=%async_computation.1 | async-start | bytes 262144 | tf_op jit(solution)/shard_map/all_to_all | solution.py:103
  119.1 3.6 %copy.48 = f32[1536,512]{0,1:T(8,128)} copy(f32[1536,512]{1,0:T(8,128)} %slice.46) | data formatting | bytes 6291456
  122.6 4.9 %add_convert_fusion = bf16[1536,512]{0,1:T(8,128)(2,1)} fusion(f32[1536,512]{0,1:T(8,128)} %copy.48, f32[1536,512]{0,1:T(8,128)} %copy.44, bf16[1536,512]{0,1:T(8,128)(2,1)S(1)} %copy.43), kind=kLoop, calls=%fused_computation.15 | loop fusion | flops 3145728 | bytes 9437184 | tf_op jit(solution)/shard_map/convert_element_type | solution.py:98
  127.6 34.0 %all-reduce.3 = (f32[512]{0:T(512)S(1)}, f32[512]{0:T(512)S(1)}) all-reduce(f32[512]{0:T(512)S(1)} %broadcast_multiply_fusion.4, f32[512]{0:T(512)S(1)} %broadcast_multiply_fusion.3), channel_id=4, replica_groups=mesh['groups'=2,'node'=16] {'node'}, use_global_device_ids=true, to_apply=%region_14.0.clone | all-reduce | flops 1024 | bytes 8192
  162.7 2.6 copy.47
  169.2 12.1 %scatter_custom_fusion.2 = f32[192,512]{1,0:T(8,128)} fusion(f32[192,512]{1,0:T(8,128)} %fusion.26, s32[1536]{0:T(1024)} %param.18, f32[1536,1536]{1,0:T(8,128)} %copy-done.4), kind=kCustom, calls=%fused_computation.10 | custom fusion | flops 786432 | bytes 3538944 | tf_op jit(solution)/shard_map/scatter-add | solution.py:102
  183.0 53.6 %reduce-scatter.9.cloned.1.call-done = f32[64,512]{1,0:T(8,128)} async-done(((f32[1024,512]{1,0:T(8,128)}), f32[64,512]{1,0:T(8,128)}) %reduce-scatter.9.cloned.1.call-update) | async-done | bytes 131088 | tf_op jit(solution)/shard_map/reduce_scatter | solution.py:124
  236.6 70.0 %reduce-scatter.5.cloned.1.call-done = f32[96,512]{1,0:T(8,128)} async-done(((f32[1536,512]{1,0:T(8,128)}), f32[96,512]{1,0:T(8,128)}) %reduce-scatter.5.cloned.1.call-update) | async-done | bytes 196624 | tf_op jit(solution)/shard_map/reduce_scatter | solution.py:118
  (124 shorter events, 35.9 us)
Async XLA Ops:
  7.2 28.9 %copy-start = (bf16[1536,512]{1,0:T(8,128)(2,1)S(1)}, bf16[1536,512]{1,0:T(8,128)(2,1)}, u32[]{:S(2)}) copy-start(bf16[1536,512]{1,0:T(8,128)(2,1)} %param.20) | copy-start | bytes 4718596
  10.6 15.7 %all-to-all-start = ((bf16[16,8,512]{2,1,0:T(8,128)(2,1)}), bf16[16,8,512]{2,1,0:T(8,128)(2,1)S(1)}, u32[]{:S(2)}, u32[]{:S(2)}) async-start(bf16[16,8,512]{2,1,0:T(8,128)(2,1)} %bitcast.1), calls=%async_computation | async-start | bytes 262144 | tf_op jit(solution)/shard_map/all_to_all | solution.py:64
  18.0 165.0 %reduce-scatter.11.cloned.1.call-start = ((), (), s32[]{:S(2)}) async-start(), calls=%async_computation.9 | async-start | bytes 1114112 | tf_op jit(solution)/shard_map/reduce_scatter | solution.py:125
  20.1 4.4 %copy-start.7 = (bf16[192,512]{1,0:T(8,128)(2,1)S(1)}, bf16[192,512]{1,0:T(8,128)(2,1)}, u32[]{:S(2)}) copy-start(bf16[192,512]{1,0:T(8,128)(2,1)} %param.13) | copy-start | bytes 589828
  20.1 4.4 %copy-start.25 = (s32[1536]{0:T(1024)S(1)}, s32[1536]{0:T(1024)}, u32[]{:S(2)}) copy-start(s32[1536]{0:T(1024)} %param.18) | copy-start | bytes 18436
  36.0 7.1 %copy-start.24 = (bf16[512,512]{1,0:T(8,128)(2,1)S(1)}, bf16[512,512]{1,0:T(8,128)(2,1)}, u32[]{:S(2)}) copy-start(bf16[512,512]{1,0:T(8,128)(2,1)} %param.21) | copy-start | bytes 1572868
  44.2 3.7 %copy-start.1 = (f32[1536,512]{0,1:T(8,128)}, f32[1536,512]{0,1:T(8,128)S(1)}, u32[]{:S(2)}) copy-start(f32[1536,512]{0,1:T(8,128)S(1)} %get-tuple-element.43) | copy-start | bytes 9437188
  44.7 3.3 %copy-start.8 = (bf16[192,512]{1,0:T(8,128)(2,1)S(1)}, bf16[192,512]{1,0:T(8,128)(2,1)}, u32[]{:S(2)}) copy-start(bf16[192,512]{1,0:T(8,128)(2,1)} %param.13) | copy-start | bytes 589828
  44.7 3.3 %copy-start.10 = (bf16[1024,512]{1,0:T(8,128)(2,1)S(1)}, bf16[1024,512]{1,0:T(8,128)(2,1)}, u32[]{:S(2)}) copy-start(bf16[1024,512]{1,0:T(8,128)(2,1)} %param.23) | copy-start | bytes 3145732
  51.7 131.3 %reduce-scatter.7.cloned.1.call-start = ((), (), s32[]{:S(2)}) async-start(), calls=%async_computation.7 | async-start | bytes 1114112 | tf_op jit(solution)/shard_map/reduce_scatter | solution.py:122
  59.9 3.6 %copy-start.30 = (f32[512]{0:T(512)S(1)}, f32[512]{0:T(512)}, u32[]{:S(2)}) copy-start(f32[512]{0:T(512)} %param.22) | copy-start | bytes 6148
  63.5 4.9 %copy-start.2 = (f32[1536,512]{0,1:T(8,128)S(1)}, f32[1536,512]{0,1:T(8,128)}, u32[]{:S(2)}) copy-start(f32[1536,512]{0,1:T(8,128)} %copy-done.1) | copy-start | bytes 9437188
  63.5 4.9 %copy-start.3 = (f32[1536,512]{0,1:T(8,128)S(1)}, f32[1536,512]{0,1:T(8,128)}, u32[]{:S(2)}) copy-start(f32[1536,512]{0,1:T(8,128)} %copy.44) | copy-start | bytes 9437188
  72.9 163.8 %reduce-scatter.9.cloned.1.call-start = ((), (), s32[]{:S(2)}) async-start(), calls=%async_computation.8 | async-start | bytes 2228224 | tf_op jit(solution)/shard_map/reduce_scatter | solution.py:124
  75.7 230.9 %reduce-scatter.5.cloned.1.call-start = ((), (), s32[]{:S(2)}) async-start(), calls=%async_computation.6 | async-start | bytes 3342336 | tf_op jit(solution)/shard_map/reduce_scatter | solution.py:118
  75.8 5.7 %copy-start.15 = (bf16[1536,512]{0,1:T(8,128)(2,1)S(1)}, bf16[1536,512]{0,1:T(8,128)(2,1)}, u32[]{:S(2)}) copy-start(bf16[1536,512]{0,1:T(8,128)(2,1)} %copy.39) | copy-start | bytes 4718596
  75.8 5.7 %copy-start.16 = (bf16[1536,512]{0,1:T(8,128)(2,1)S(1)}, bf16[1536,512]{0,1:T(8,128)(2,1)}, u32[]{:S(2)}) copy-start(bf16[1536,512]{0,1:T(8,128)(2,1)} %convolution_convert_fusion) | copy-start | bytes 4718596
  75.8 5.7 %copy-start.17 = (bf16[1536,512]{0,1:T(8,128)(2,1)S(1)}, bf16[1536,512]{0,1:T(8,128)(2,1)}, u32[]{:S(2)}) copy-start(bf16[1536,512]{0,1:T(8,128)(2,1)} %copy.42) | copy-start | bytes 4718596
  94.5 3.6 %copy-start.4 = (f32[1536,1536]{1,0:T(8,128)}, f32[1536,1536]{1,0:T(8,128)S(1)}, u32[]{:S(2)}) copy-start(f32[1536,1536]{1,0:T(8,128)S(1)} %fusion.45) | copy-start | bytes 28311556
  113.0 52.3 %all-to-all-start.1 = ((bf16[16,8,512]{2,1,0:T(8,128)(2,1)}), bf16[16,8,512]{2,1,0:T(8,128)(2,1)}, u32[]{:S(2)}, u32[]{:S(2)}) async-start(bf16[16,8,512]{2,1,0:T(8,128)(2,1)} %fusion.33), calls=%async_computation.1 | async-start | bytes 262144 | tf_op jit(solution)/shard_map/all_to_all | solution.py:103
  122.6 4.9 %copy-start.27 = (f32[512]{0:T(512)S(1)}, f32[512]{0:T(512)}, u32[]{:S(2)}) copy-start(f32[512]{0:T(512)} %get-tuple-element.35) | copy-start | bytes 6148
  122.6 4.9 %copy-start.28 = (f32[512]{0:T(512)S(1)}, f32[512]{0:T(512)}, u32[]{:S(2)}) copy-start(f32[512]{0:T(512)} %get-tuple-element.32) | copy-start | bytes 6148
  127.6 39.8 %copy-start.12 = (f32[192,1024]{1,0:T(8,128)S(1)}, f32[192,1024]{1,0:T(8,128)}, u32[]{:S(2)}) copy-start(f32[192,1024]{1,0:T(8,128)} %copy-done.11) | copy-start | bytes 2359300
  127.6 39.8 %copy-start.13 = (f32[320,512]{1,0:T(8,128)S(1)}, f32[320,512]{1,0:T(8,128)}, u32[]{:S(2)}) copy-start(f32[320,512]{1,0:T(8,128)} %scatter_custom_fusion) | copy-start | bytes 1966084
  (17 other events, 25.8 us)
Sparse Core Ops, SparseCore 0:
  51.9 58.7 reduce-scatter.10
  115.2 56.3 reduce-scatter.6
  176.0 60.5 reduce-scatter.8
  241.3 65.2 reduce-scatter.4
where the time goes:
time: 314 us; the launch traced here: 313 us
  waiting for transfers between devices  124 us (39%)
  local copies, waits for them, and re-layouts  46.4 us (15%)
  other arithmetic  45.2 us (14%)
  matrix products  35.3 us (11%)
  blocking collectives  34 us (11%)
  between operations  14.8 us (5%)
  starting transfers between devices  13.8 us (4%)
    reduce_scatter x1, waiting for transfers between devices, local(): lax.psum_scatter(contract_rows(edge_input, edge_agrad) * edge_scale, 'nod...  70 us
    reduce_scatter x1, waiting for transfers between devices, local(): lax.psum_scatter(node_w1_part, 'node', scatter_dimension=0, tiled=True)  53.6 us
    unnamed x1, blocking collectives  34 us
    unnamed x78, local copies, waits for them, and re-layouts  22.7 us
    dot_general x5, matrix products, contract_rows(): lax.dot_general(left, right, (((0,), (0,)), ((), ())), preferred_element_...  13.9 us
    scatter-add x1, other arithmetic, local(): jax.ops.segment_sum(edge_xgrad[:, 2 * width:], receiver, num_segments=nod...  12.1 us
    scatter-add x1, other arithmetic, local(): jax.ops.segment_sum(edge_xgrad[:, width:2 * width], sender_slot, num_segm...  11.3 us
    dot_general x4, matrix products, contract_cols(): lax.dot_general(left, right, (((1,), (1,)), ((), ())), preferred_element_...  10.7 us
  transfers between devices with their start and end apart: 6, of which 2 were waited for; matrix products, arithmetic and copies ran while one was open for 29% of the time, Pallas kernels for 0%

commit v1 on v0

v1 whole, which is shorter than its diff:
```python
import functools
import math

import jax
import jax.numpy as jnp
from jax import lax
from jax.experimental import pallas as pl
from jax.experimental.pallas import tpu as pltpu
from jax.sharding import PartitionSpec as P

F32 = jnp.float32
BF16 = jnp.bfloat16
MESH = pl.DeviceIdType.MESH
VMEM_LIMIT = 56 * 1024 * 1024
CHUNK = 256


def mm(left, right):
    return jnp.dot(left, right, preferred_element_type=F32)


def mm_rows(left, right):
    return lax.dot_general(left, right, (((0,), (0,)), ((), ())), preferred_element_type=F32)


def mm_cols(left, right):
    return lax.dot_general(left, right, (((1,), (1,)), ((), ())), preferred_element_type=F32)


def pack(rows):
    cap, half = rows.shape[1], rows.shape[2] // 2
    return jnp.concatenate([rows[:, :, :half], rows[:, :, half:]], axis=1).astype(BF16)


def unpack(packed):
    n, cap = packed.shape[0], packed.shape[1] // 2
    wide = packed.astype(F32)
    both = jnp.concatenate([wide[:, :cap, :], wide[:, cap:, :]], axis=2)
    return both.reshape(n * cap, both.shape[2])


def swap_blocks(n, me, src, dst, send_sem, recv_sem):
    def copy_to(peer):
        return pltpu.make_async_remote_copy(
            src_ref=src.at[peer],
            dst_ref=dst.at[me],
            send_sem=send_sem.at[peer],
            recv_sem=recv_sem.at[me],
            device_id={"node": peer},
            device_id_type=MESH,
        )

    def copy_from(peer):
        return pltpu.make_async_remote_copy(
            src_ref=src.at[peer],
            dst_ref=dst.at[peer],
            send_sem=send_sem.at[peer],
            recv_sem=recv_sem.at[peer],
            device_id={"node": peer},
            device_id_type=MESH,
        )

    def start():
        @pl.loop(1, n)
        def _(k):
            copy_to(lax.rem(me + k, n)).start()

    def wait_recv():
        @pl.loop(1, n)
        def _(k):
            copy_from(lax.rem(me + k, n)).wait_recv()

    def wait_send():
        @pl.loop(1, n)
        def _(k):
            copy_from(lax.rem(me + k, n)).wait_send()

    return start, wait_recv, wait_send


def greet_all(n, me):
    barrier = pltpu.get_barrier_semaphore()

    @pl.loop(1, n)
    def _(k):
        pl.semaphore_signal(
            barrier, inc=1, device_id={"node": lax.rem(me + k, n)}, device_id_type=MESH
        )

    pl.semaphore_wait(barrier, n - 1)


def halo_kernel(n, index_ref, node_ref, in_ref, out_buf, in_buf, send_sem, recv_sem):
    me = lax.axis_index("node")
    nodes = node_ref.shape[0]
    slots = index_ref.shape[0]
    pick = (
        index_ref[...] == lax.broadcasted_iota(jnp.int32, (slots, nodes), 1)
    ).astype(F32).astype(BF16)
    rows = mm(pick, node_ref[...])
    out_buf[...] = pack(rows.reshape(n, slots // n, rows.shape[1]))
    in_buf[me] = jnp.zeros(in_buf.shape[1:], BF16)
    greet_all(n, me)
    start, wait_recv, wait_send = swap_blocks(n, me, out_buf, in_buf, send_sem, recv_sem)
    start()
    wait_recv()
    in_ref[...] = in_buf[...]
    wait_send()


def norm_back(grad, normed, inverse, gain):
    scaled = grad * gain
    first = jnp.mean(scaled, axis=-1, keepdims=True)
    second = jnp.mean(scaled * normed, axis=-1, keepdims=True)
    return inverse * (scaled - first - normed * second)


def normalize(values):
    mean = jnp.mean(values, axis=-1, keepdims=True)
    centred = values - mean
    inverse = lax.rsqrt(jnp.mean(centred * centred, axis=-1, keepdims=True) + 1e-05)
    return centred * inverse, inverse


def silu_parts(pre):
    sig = jax.nn.sigmoid(pre)
    return (pre * sig).astype(BF16), sig * (1.0 + pre * (1.0 - sig))


def bit_orders(n):
    bits = n.bit_length() - 1
    cut = 1 + (bits - 1) // 2
    low, high = list(range(1, cut)), list(range(cut, bits))
    return [0] + low + high, [0] + high + low


def place_of(d, order):
    place = 0
    for bit in order:
        place = 2 * place + ((d >> bit) & 1)
    return place


def layer_kernel(
    n,
    rows_of,
    node_scale,
    edge_scale,
    node_ref,
    halo_ref,
    latent_ref,
    node_cot_ref,
    cot_ref,
    send_col,
    recv_col,
    send_row,
    recv_row,
    w1_ref,
    w2_ref,
    gain_ref,
    nw1_ref,
    nw2_ref,
    ngain_ref,
    edge_out,
    first_out,
    second_out,
    slot_out,
    base_out,
    table,
    proj,
    pick,
    pick_t,
    slope,
    hidden,
    hat,
    inv,
    rows_bf,
    agrad,
    agg_bf,
    gain_sum,
    grad_w1,
    grad_w2,
    grad_n1,
    grad_n2,
):
    nodes, width = node_ref.shape
    edges = latent_ref.shape[0]
    slots = table.shape[0]
    total_cols = slots + nodes
    steps = edges // CHUNK
    node = node_ref[...]
    table[:nodes, :] = node
    table[nodes:, :] = unpack(halo_ref[...]).astype(BF16)
    proj[:slots, :] = mm(table[...], w1_ref[width : 2 * width, :]).astype(BF16)
    proj[slots:, :] = mm(node, w1_ref[2 * width :, :]).astype(BF16)

    row_id = lax.broadcasted_iota(jnp.int32, (slots, edges), 0)
    pick_t[:slots, :] = (row_id == send_row[...]).astype(F32).astype(BF16)
    row_id = lax.broadcasted_iota(jnp.int32, (nodes, edges), 0)
    pick_t[slots:, :] = (row_id == recv_row[...]).astype(F32).astype(BF16)

    @pl.loop(0, steps)
    def _(step):
        here = pl.ds(pl.multiple_of(step * CHUNK, CHUNK), CHUNK)
        col_id = lax.broadcasted_iota(jnp.int32, (CHUNK, total_cols), 1)
        chosen = (col_id == send_col[here, :]) | (col_id == recv_col[here, :] + slots)
        one_hot = chosen.astype(F32).astype(BF16)
        pick[here, :] = one_hot
        latent = latent_ref[here, :]
        pre = mm(latent, w1_ref[:width, :]) + mm(one_hot, proj[...])
        hid, slope_here = silu_parts(pre)
        hidden[here, :] = hid
        slope[here, :] = slope_here
        hat_here, inv_here = normalize(mm(hid, w2_ref[...]))
        hat[here, :] = hat_here
        inv[here, :] = inv_here
        rows_bf[here, :] = (latent.astype(F32) + hat_here * gain_ref[...]).astype(BF16)

    aggregate = mm(pick_t[slots:, :], rows_bf[...]).astype(BF16)
    node_pre = mm(node, nw1_ref[:width, :]) + mm(aggregate, nw1_ref[width:, :])
    node_hidden, node_slope = silu_parts(node_pre)
    node_hat, node_inv = normalize(mm(node_hidden, nw2_ref[...]))
    node_dy = node_cot_ref[...].astype(F32)
    node_gain_part = jnp.sum(node_dy * node_hat, axis=0, keepdims=True) * node_scale
    node_mgrad = norm_back(node_dy, node_hat, node_inv, ngain_ref[...]).astype(BF16)
    grad_n2[...] = mm_rows(node_hidden, node_mgrad)
    node_agrad = (mm_cols(node_mgrad, nw2_ref[...]) * node_slope).astype(BF16)
    grad_n1[:width, :] = mm_rows(node, node_agrad)
    grad_n1[width:, :] = mm_rows(aggregate, node_agrad)
    agg_bf[...] = mm_cols(node_agrad, nw1_ref[width:, :]).astype(BF16)
    base_out[...] = node_dy + mm_cols(node_agrad, nw1_ref[:width, :])
    gain_sum[...] = jnp.zeros_like(gain_sum)

    @pl.loop(0, steps)
    def _(step):
        here = pl.ds(pl.multiple_of(step * CHUNK, CHUNK), CHUNK)
        col_id = lax.broadcasted_iota(jnp.int32, (CHUNK, nodes), 1)
        incidence = (col_id == recv_col[here, :]).astype(F32).astype(BF16)
        total = cot_ref[here, :].astype(F32) + mm(incidence, agg_bf[...])
        hat_here = hat[here, :]
        product = total * hat_here
        gain_sum[...] += jnp.sum(product.reshape(CHUNK // 8, 8, width), axis=0)
        mgrad = norm_back(total, hat_here, inv[here, :], gain_ref[...]).astype(BF16)
        rows_bf[here, :] = mgrad
        ag = (mm_cols(mgrad, w2_ref[...]) * slope[here, :]).astype(BF16)
        agrad[here, :] = ag
        edge_out[here, :] = (total + mm_cols(ag, w1_ref[:width, :])).astype(BF16)

    edge_gain_part = jnp.sum(gain_sum[...], axis=0, keepdims=True) * edge_scale
    grad_w2[...] = mm_rows(hidden[...], rows_bf[...])
    grad_w1[:width, :] = mm_rows(latent_ref[...], agrad[...])
    sums = mm(pick_t[...], agrad[...]).astype(BF16)
    by_slot, by_target = sums[:slots, :], sums[slots:, :]
    grad_w1[width : 2 * width, :] = mm_rows(table[...], by_slot)
    grad_w1[2 * width :, :] = mm_rows(node, by_target)
    slot_sums = mm_cols(by_slot, w1_ref[width : 2 * width, :])
    base_out[...] += slot_sums[:nodes, :] + mm_cols(by_target, w1_ref[2 * width :, :])
    remote = slot_sums[nodes:, :]
    slot_out[...] = pack(remote.reshape(n, remote.shape[0] // n, width))

    half = width // 2
    used = sum(rows_of)
    spare = first_out.shape[1] - used
    row_id = lax.broadcasted_iota(jnp.int32, (spare, width), 0)
    tail = jnp.where(row_id == 0, edge_gain_part, jnp.where(row_id == 1, node_gain_part, 0.0))
    sources = (
        (grad_w1, edge_scale),
        (grad_w2, edge_scale),
        (grad_n1, node_scale),
        (grad_n2, node_scale),
    )
    for order, out, cols in zip(
        bit_orders(n), (first_out, second_out), (slice(0, half), slice(half, width))
    ):
        for d in range(n):
            pieces = []
            for (source, scale), rows in zip(sources, rows_of):
                pieces.append(source[d * rows : (d + 1) * rows, cols] * scale)
            pieces.append(tail[:, cols])
            out[place_of(d, order)] = jnp.concatenate(pieces, axis=0).astype(BF16)


def sum_kernel(
    n,
    rows_of,
    first_ref,
    second_ref,
    slot_ref,
    base_ref,
    index_ref,
    node_out,
    w1_out,
    w2_out,
    n1_out,
    n2_out,
    gain_out,
    *scratch,
):
    me = lax.axis_index("node")
    bits = n.bit_length() - 1
    held = [first_ref, second_ref]
    landing = (scratch[:bits], scratch[bits : 2 * bits])
    slot_in, send_sem, recv_sem, halo_send, halo_recv = scratch[2 * bits :]
    greet_all(n, me)
    start, wait_recv, wait_send = swap_blocks(n, me, slot_ref, slot_in, halo_send, halo_recv)
    orders = bit_orders(n)
    copies = {}
    bases = [0, 0]

    def launch(path, level):
        bit = orders[path][level]
        mine = lax.rem(me // (1 << bit), 2)
        size = n >> (level + 1)
        peer = me + (1 - 2 * mine) * (1 << bit)
        source = held[path].at[pl.ds(bases[path] + (1 - mine) * size, size)]
        bases[path] = bases[path] + mine * size
        copy = pltpu.make_async_remote_copy(
            src_ref=source,
            dst_ref=landing[path][level],
            send_sem=send_sem.at[path, level],
            recv_sem=recv_sem.at[path, level],
            device_id={"node": peer},
            device_id_type=MESH,
        )
        copy.start()
        copies[path, level] = copy

    launch(0, 0)
    launch(1, 0)
    start()
    half = first_ref.shape[2]
    for level in range(bits):
        for path in range(2):
            copies[path, level].wait_recv()
            size = n >> (level + 1)
            base = bases[path]
            if level < bits - 1:

                @pl.loop(0, size)
                def _(k):
                    landing[path][level][k] = (
                        held[path][base + k].astype(F32) + landing[path][level][k].astype(F32)
                    ).astype(BF16)

                held[path] = landing[path][level]
                bases[path] = 0
                launch(path, level + 1)
            else:
                cols = slice(path * half, (path + 1) * half)
                done = held[path][base].astype(F32) + landing[path][level][0].astype(F32)
                at = 0
                for out, rows in zip((w1_out, w2_out, n1_out, n2_out), rows_of):
                    out[:, cols] = done[at : at + rows, :]
                    at += rows
                gain_out[:, cols] = done[at : at + 2, :]
    slot_in[me] = jnp.zeros(slot_in.shape[1:], BF16)
    wait_recv()
    nodes = base_ref.shape[0]
    slots = index_ref.shape[1]
    owner = (
        lax.broadcasted_iota(jnp.int32, (nodes, slots), 0) == index_ref[...]
    ).astype(F32).astype(BF16)
    back = mm(owner, unpack(slot_in[...]).astype(BF16))
    node_out[...] = (base_ref[...] + back).astype(BF16)
    for copy in copies.values():
        copy.wait_send()
    wait_send()


def local(
    n,
    node_latent,
    edge_latent,
    node_cotangent,
    edge_cotangent,
    sender_slot,
    receiver,
    send_index,
    edge_w1,
    edge_w2,
    edge_gain,
    node_w1,
    node_w2,
    node_gain,
):
    nodes, width = node_latent.shape
    edges = edge_latent.shape[0]
    cap = send_index.shape[2]
    half = width // 2
    bits = n.bit_length() - 1
    node_scale = 1.0 / math.sqrt(nodes * n)
    edge_scale = 1.0 / math.sqrt(edges * n)
    rows_of = tuple(w.shape[0] // n for w in (edge_w1, edge_w2, node_w1, node_w2))
    block = -(-(sum(rows_of) + 2) // 16) * 16
    slots = nodes + n * cap
    vmem = pl.BlockSpec(memory_space=pltpu.VMEM)
    packed = jax.ShapeDtypeStruct((n, 2 * cap, half), BF16)
    stack = jax.ShapeDtypeStruct((n, block, half), BF16)

    incoming = pl.pallas_call(
        functools.partial(halo_kernel, n),
        out_shape=packed,
        in_specs=[vmem] * 2,
        out_specs=vmem,
        scratch_shapes=[
            pltpu.VMEM(packed.shape, BF16),
            pltpu.VMEM(packed.shape, BF16),
            pltpu.SemaphoreType.DMA((n,)),
            pltpu.SemaphoreType.DMA((n,)),
        ],
        compiler_params=pltpu.CompilerParams(
            collective_id=0, has_side_effects=True, vmem_limit_bytes=VMEM_LIMIT
        ),
    )(send_index.reshape(n * cap, 1), node_latent)

    edge_grad, first, second, slot_sums, base = pl.pallas_call(
        functools.partial(layer_kernel, n, rows_of, node_scale, edge_scale),
        out_shape=(
            jax.ShapeDtypeStruct((edges, width), BF16),
            stack,
            stack,
            packed,
            jax.ShapeDtypeStruct((nodes, width), F32),
        ),
        in_specs=[vmem] * 15,
        out_specs=(vmem,) * 5,
        scratch_shapes=[
            pltpu.VMEM((slots, width), BF16),
            pltpu.VMEM((slots + nodes, width), BF16),
            pltpu.VMEM((edges, slots + nodes), BF16),
            pltpu.VMEM((slots + nodes, edges), BF16),
            pltpu.VMEM((edges, width), F32),
            pltpu.VMEM((edges, width), BF16),
            pltpu.VMEM((edges, width), F32),
            pltpu.VMEM((edges, 1), F32),
            pltpu.VMEM((edges, width), BF16),
            pltpu.VMEM((edges, width), BF16),
            pltpu.VMEM((nodes, width), BF16),
            pltpu.VMEM((8, width), F32),
            pltpu.VMEM((3 * width, width), F32),
            pltpu.VMEM((width, width), F32),
            pltpu.VMEM((2 * width, width), F32),
            pltpu.VMEM((width, width), F32),
        ],
        compiler_params=pltpu.CompilerParams(vmem_limit_bytes=VMEM_LIMIT),
    )(
        node_latent,
        incoming,
        edge_latent,
        node_cotangent,
        edge_cotangent,
        sender_slot.reshape(edges, 1),
        receiver.reshape(edges, 1),
        sender_slot.reshape(1, edges),
        receiver.reshape(1, edges),
        edge_w1,
        edge_w2,
        edge_gain.reshape(1, width),
        node_w1,
        node_w2,
        node_gain.reshape(1, width),
    )

    landing = [pltpu.VMEM((n >> (level + 1), block, half), BF16) for level in range(bits)]
    node_grad, w1_grad, w2_grad, n1_grad, n2_grad, gains = pl.pallas_call(
        functools.partial(sum_kernel, n, rows_of),
        out_shape=(jax.ShapeDtypeStruct((nodes, width), BF16),)
        + tuple(jax.ShapeDtypeStruct((rows, width), F32) for rows in rows_of)
        + (jax.ShapeDtypeStruct((2, width), F32),),
        in_specs=[vmem] * 5,
        out_specs=(vmem,) * 6,
        scratch_shapes=landing
        + landing
        + [
            pltpu.VMEM(packed.shape, BF16),
            pltpu.SemaphoreType.DMA((2, bits)),
            pltpu.SemaphoreType.DMA((2, bits)),
            pltpu.SemaphoreType.DMA((n,)),
            pltpu.SemaphoreType.DMA((n,)),
        ],
        compiler_params=pltpu.CompilerParams(
            collective_id=1, has_side_effects=True, vmem_limit_bytes=VMEM_LIMIT
        ),
    )(first, second, slot_sums, base, send_index.reshape(1, n * cap))
    share = width // n
    own = lax.dynamic_slice(gains, (0, lax.axis_index("node") * share), (2, share))
    return node_grad, edge_grad, w1_grad, w2_grad, own[0], n1_grad, n2_grad, own[1]


def solution(mesh):
    rows = P(("groups", "node"), None)
    flat = P(("groups", "node"))
    return jax.shard_map(
        functools.partial(local, mesh.shape["node"]),
        mesh=mesh,
        in_specs=(rows, rows, rows, rows, flat, flat, P(("groups", "node"), None, None))
        + (P(),) * 6,
        out_specs=(rows, rows, rows, rows, flat, rows, rows, flat),
        check_vma=False,
    )
```

time: 314 us -> 96.7 us (0.31)
  waiting for transfers between devices: 124 us -> 0 us
  Pallas kernels: 0 us -> 78.2 us
  other arithmetic: 45.2 us -> 0 us
  matrix products: 35.3 us -> 0 us
  blocking collectives: 34 us -> 0 us
  local copies, waits for them, and re-layouts: 46.4 us -> 17.4 us
  between operations: 14.8 us -> 0.66 us
  starting transfers between devices: 13.8 us -> 0 us
    reduce_scatter x4 -> x0, waiting for transfers between devices: 124 us -> none  [the longest x1 70 us: local(): lax.psum_scatter(contract_rows(edge_input, edge_agrad) * edge_scale, 'nod...]
    pallas_call x0 -> x3, Pallas kernels: none -> 78.2 us  [the longest x1 42.2 us: local(): pl.pallas_call(functools.partial(sum_kernel, n, rows_of), out_shape=(jax....]
    dot_general x14 -> x0, matrix products: 35.3 us -> none  [the longest x5 13.9 us: contract_rows(): lax.dot_general(left, right, (((0,), (0,)), ((), ())), preferred_element_...]
    unnamed x1 -> x0, blocking collectives: 34 us -> none
    scatter-add x3 -> x0, other arithmetic: 25.5 us -> none  [the longest x1 12.1 us: local(): jax.ops.segment_sum(edge_xgrad[:, 2 * width:], receiver, num_segments=nod...]
    gather x5 -> x0, local copies, waits for them, and re-layouts: 18.4 us -> none  [the longest x2 8.88 us: local(): node_xgrad[:, width:][receiver]]
    unnamed x78 -> x6, local copies, waits for them, and re-layouts: 22.7 us -> 8.5 us
    all_to_all x2 -> x0, starting transfers between devices: 13.5 us -> none  [the longest x1 7.39 us: local(): lax.all_to_all(outgoing, 'node', split_axis=0, concat_axis=0, tiled=True)]
  transfers between devices with their start and end apart: 6 -> 0, of which waited for: 2 -> 0; matrix products, arithmetic and copies ran while one was open for 29% -> 0% of each run, Pallas kernels for 0% -> 0%
where the time goes in v1:
time: 96.7 us; the launch traced here: 96.2 us
  Pallas kernels  78.2 us (81%)
  local copies, waits for them, and re-layouts  17.4 us (18%)
    pallas_call x1, Pallas kernels, local(): pl.pallas_call(functools.partial(sum_kernel, n, rows_of), out_shape=(jax....  42.2 us
    pallas_call x1, Pallas kernels, local(): pl.pallas_call(functools.partial(layer_kernel, n, rows_of, node_scale, ed...  24.4 us
    pallas_call x1, Pallas kernels, local(): pl.pallas_call(functools.partial(halo_kernel, n), out_shape=packed, in_sp...  11.6 us
    unnamed x6, local copies, waits for them, and re-layouts  8.5 us

profile of v1, /device:TPU:0, one launch (start us, length us, event | category | flops | bytes accessed | tf_op | source)
XLA Modules:
  0.0 96.2 jit_solution(2412515378087972728)
XLA Ops:
  0.6 1.3 %reshape.43.send_row = s32[1,1536]{1,0:T(1,128)} reshape(s32[1536]{0:T(1024)} %param.17) | data formatting | bytes 12288 | tf_op jit(solution)/shard_map/reshape | solution.py:454
  1.9 1.3 %reshape.44.recv_row = s32[1,1536]{1,0:T(1,128)} reshape(s32[1536]{0:T(1024)} %param.18) | data formatting | bytes 12288 | tf_op jit(solution)/shard_map/reshape | solution.py:455
  3.2 0.8 copy.24
  4.0 0.6 reshape.47.index_ref
  4.6 0.7 reshape.48.index_ref
  5.3 11.6 %shard_map.188.halo_ref = bf16[16,16,256]{2,1,0:T(8,128)(2,1)} custom-call(s32[128,1]{1,0:T(8,128)} %reshape.48.index_ref, bf16[192,512]{1,0:T(8,128)(2,1)} %node_ref.3), custom_call_target="tpu_custom_call" | custom-call | tf_op jit(solution)/shard_map/pallas_call | solution.py:400
  16.9 1.9 %reshape.49.send_col = s32[1536,1]{1,0:T(8,128)} reshape(s32[1536]{0:T(1024)} %param.17) | data formatting | bytes 12288 | tf_op jit(solution)/shard_map/reshape | solution.py:452
  18.7 1.9 %reshape.50.recv_col = s32[1536,1]{1,0:T(8,128)} reshape(s32[1536]{0:T(1024)} %param.18) | data formatting | bytes 12288 | tf_op jit(solution)/shard_map/reshape | solution.py:453
  20.6 24.4 %shard_map.189 = (bf16[1536,512]{1,0:T(8,128)(2,1)}, bf16[16,240,256]{2,1,0:T(8,128)(2,1)}, bf16[16,240,256]{2,1,0:T(8,128)(2,1)}, bf16[16,16,256]{2,1,0:T(8,128)(2,1)}, f32[192,512]{1,0:T(8,128)}) custom-call(bf16[192,512]{1,0:T(8,128)(2,1)} %node_ref.3, bf16[16,16,256]{2,1,0:T(8,128)(2,1)} %shard_map.188.halo_ref, bf16[1536,512]{1,0:T(8,128)(2,1)} %latent_ref.1, ...), custom_call_target="tpu_custom_call" | custom-call | tf_op jit(solution)/shard_map/pallas_call | solution.py:416
  45.0 42.2 %shard_map.190 = (bf16[192,512]{1,0:T(8,128)(2,1)}, f32[96,512]{1,0:T(8,128)}, f32[32,512]{1,0:T(8,128)}, f32[64,512]{1,0:T(8,128)}, f32[32,512]{1,0:T(8,128)}, /*index=5*/f32[2,512]{1,0:T(2,128)}) custom-call(bf16[16,240,256]{2,1,0:T(8,128)(2,1)} %get-tuple-element.19.first_ref, bf16[16,240,256]{2,1,0:T(8,128)(2,1)} %get-tuple-element.20.second_ref, ...), custom_call_target="tpu_custom_call" | custom-call | tf_op jit(solution)/shard_map/pallas_call | solution.py:465
  87.2 0.7 constant_dynamic-slice_fusion
  87.9 0.5 slice_bitcast_fusion
  88.5 1.6 %copy.34 = bf16[192,512]{1,0:T(8,128)(2,1)} copy(bf16[192,512]{1,0:T(8,128)(2,1)} %get-tuple-element.40) | data formatting | bytes 393216
  90.1 1.6 %copy.35 = f32[96,512]{1,0:T(8,128)} copy(f32[96,512]{1,0:T(8,128)} %get-tuple-element.42) | data formatting | bytes 393216
  91.7 1.5 %copy.36 = f32[32,512]{1,0:T(8,128)} copy(f32[32,512]{1,0:T(8,128)} %get-tuple-element.43) | data formatting | bytes 131072
  93.2 1.6 %copy.37 = f32[64,512]{1,0:T(8,128)} copy(f32[64,512]{1,0:T(8,128)} %get-tuple-element.45) | data formatting | bytes 262144
  94.7 1.5 %copy.38 = f32[32,512]{1,0:T(8,128)} copy(f32[32,512]{1,0:T(8,128)} %get-tuple-element.46) | data formatting | bytes 131072

commit v2 on v1

v2 whole, which is shorter than its diff:
```python
import functools
import math

import jax
import jax.numpy as jnp
from jax import lax
from jax.experimental import pallas as pl
from jax.experimental.pallas import tpu as pltpu
from jax.sharding import PartitionSpec as P

F32 = jnp.float32
BF16 = jnp.bfloat16
MESH = pl.DeviceIdType.MESH
VMEM_LIMIT = 56 * 1024 * 1024
CHUNK = 256


def mm(left, right):
    return jnp.dot(left, right, preferred_element_type=F32)


def mm_rows(left, right):
    return lax.dot_general(left, right, (((0,), (0,)), ((), ())), preferred_element_type=F32)


def mm_cols(left, right):
    return lax.dot_general(left, right, (((1,), (1,)), ((), ())), preferred_element_type=F32)


def pack(rows):
    cap, half = rows.shape[1], rows.shape[2] // 2
    return jnp.concatenate([rows[:, :, :half], rows[:, :, half:]], axis=1).astype(BF16)


def unpack(packed):
    n, cap = packed.shape[0], packed.shape[1] // 2
    wide = packed.astype(F32)
    both = jnp.concatenate([wide[:, :cap, :], wide[:, cap:, :]], axis=2)
    return both.reshape(n * cap, both.shape[2])


def swap_blocks(n, me, src, dst, send_sem, recv_sem):
    def copy_to(peer):
        return pltpu.make_async_remote_copy(
            src_ref=src.at[peer],
            dst_ref=dst.at[me],
            send_sem=send_sem.at[peer],
            recv_sem=recv_sem.at[me],
            device_id={"node": peer},
            device_id_type=MESH,
        )

    def copy_from(peer):
        return pltpu.make_async_remote_copy(
            src_ref=src.at[peer],
            dst_ref=dst.at[peer],
            send_sem=send_sem.at[peer],
            recv_sem=recv_sem.at[peer],
            device_id={"node": peer},
            device_id_type=MESH,
        )

    def start():
        @pl.loop(1, n)
        def _(k):
            copy_to(lax.rem(me + k, n)).start()

    def wait_recv():
        @pl.loop(1, n)
        def _(k):
            copy_from(lax.rem(me + k, n)).wait_recv()

    def wait_send():
        @pl.loop(1, n)
        def _(k):
            copy_from(lax.rem(me + k, n)).wait_send()

    return start, wait_recv, wait_send


def greet_all(n, me):
    barrier = pltpu.get_barrier_semaphore()

    @pl.loop(1, n)
    def _(k):
        pl.semaphore_signal(
            barrier, inc=1, device_id={"node": lax.rem(me + k, n)}, device_id_type=MESH
        )

    return barrier


def norm_back(grad, normed, inverse, gain):
    scaled = grad * gain
    first = jnp.mean(scaled, axis=-1, keepdims=True)
    second = jnp.mean(scaled * normed, axis=-1, keepdims=True)
    return inverse * (scaled - first - normed * second)


def normalize(values):
    mean = jnp.mean(values, axis=-1, keepdims=True)
    centred = values - mean
    inverse = lax.rsqrt(jnp.mean(centred * centred, axis=-1, keepdims=True) + 1e-05)
    return centred * inverse, inverse


def silu_parts(pre):
    sig = jax.nn.sigmoid(pre)
    return (pre * sig).astype(BF16), sig * (1.0 + pre * (1.0 - sig))


def bit_orders(n):
    bits = n.bit_length() - 1
    cut = 1 + (bits - 1) // 2
    low, high = list(range(1, cut)), list(range(cut, bits))
    return [0] + low + high, [0] + high + low


def place_of(d, order):
    place = 0
    for bit in order:
        place = 2 * place + ((d >> bit) & 1)
    return place


def layer_kernel(
    n,
    waves,
    node_scale,
    edge_scale,
    index_ref,
    node_ref,
    latent_ref,
    node_cot_ref,
    cot_ref,
    w1_ref,
    w2_ref,
    gain_ref,
    nw1_ref,
    nw2_ref,
    ngain_ref,
    edge_out,
    base_out,
    slot_out,
    node_sum_out,
    w2_sum_out,
    w1_sum_out,
    halo_out,
    halo_in,
    slot_send,
    slot_in,
    table,
    proj,
    pick_t,
    slope,
    hidden,
    hat,
    inv,
    rows_bf,
    agrad,
    agg_bf,
    gain_sum,
    grad_w1,
    grad_w2,
    out_send,
    out_recv,
    back_send,
    back_recv,
    wave_send,
    wave_recv,
    *buffers,
):
    me = lax.axis_index("node")
    barrier = greet_all(n, me)
    grad_n1, grad_n2 = grad_w1, grad_w2
    nodes, width = node_ref.shape
    half = width // 2
    edges = latent_ref.shape[0]
    slots = table.shape[0]
    halo = slots - nodes
    steps = edges // CHUNK
    bits = n.bit_length() - 1
    orders = bit_orders(n)
    stacks = [[buffers[2 * w + p] for p in range(2)] for w in range(3)]
    rest = buffers[6:]
    landing = [
        [[rest[(2 * w + p) * bits + level] for level in range(bits)] for p in range(2)]
        for w in range(3)
    ]
    held = [list(pair) for pair in stacks]
    bases = [[0, 0] for _ in range(3)]
    copies = {}

    def launch(w, path, level):
        bit = orders[path][level]
        mine = lax.rem(me // (1 << bit), 2)
        size = n >> (level + 1)
        peer = me + (1 - 2 * mine) * (1 << bit)
        source = held[w][path].at[pl.ds(bases[w][path] + (1 - mine) * size, size)]
        bases[w][path] = bases[w][path] + mine * size
        copy = pltpu.make_async_remote_copy(
            src_ref=source,
            dst_ref=landing[w][path][level],
            send_sem=wave_send.at[w, path, level],
            recv_sem=wave_recv.at[w, path, level],
            device_id={"node": peer},
            device_id_type=MESH,
        )
        copy.start()
        copies[w, path, level] = copy

    def advance(w, level):
        for path in range(2):
            copies[w, path, level].wait_recv()
            size = n >> (level + 1)
            base = bases[w][path]
            kept, came = held[w][path], landing[w][path][level]
            if level < bits - 1:

                @pl.loop(0, size)
                def _(k):
                    came[k] = (kept[base + k].astype(F32) + came[k].astype(F32)).astype(BF16)

                held[w][path] = came
                bases[w][path] = 0
                launch(w, path, level + 1)
            else:
                cols = slice(path * half, (path + 1) * half)
                out = (node_sum_out, w2_sum_out, w1_sum_out)[w]
                out[:, cols] = kept[base].astype(F32) + came[0].astype(F32)

    def fill(w, sources, tail):
        for path in range(2):
            cols = slice(path * half, (path + 1) * half)
            out = stacks[w][path]
            spare = out.shape[1] - sum(rows for _, _, rows in sources)
            for d in range(n):
                pieces = []
                for source, scale, rows in sources:
                    pieces.append(source[d * rows : (d + 1) * rows, cols] * scale)
                if spare:
                    pieces.append(tail[:spare, cols])
                out[place_of(d, orders[path])] = jnp.concatenate(pieces, axis=0).astype(BF16)
            launch(w, path, 0)

    node = node_ref[...]
    owner = (
        lax.broadcasted_iota(jnp.int32, (nodes, halo), 0) == index_ref[:, 2 * edges :]
    ).astype(F32).astype(BF16)
    halo_out[...] = pack(mm_rows(owner, node).reshape(n, halo // n, width))
    halo_in[me] = jnp.zeros(halo_in.shape[1:], BF16)
    slot_in[me] = jnp.zeros(slot_in.shape[1:], BF16)
    pl.semaphore_wait(barrier, n - 1)
    start, wait_in, wait_out = swap_blocks(n, me, halo_out, halo_in, out_send, out_recv)
    start()

    row_id = lax.broadcasted_iota(jnp.int32, (slots, edges), 0)
    pick_t[:slots, :] = (row_id == index_ref[:, :edges]).astype(F32).astype(BF16)
    row_id = lax.broadcasted_iota(jnp.int32, (nodes, edges), 0)
    pick_t[slots:, :] = (row_id == index_ref[:, edges : 2 * edges]).astype(F32).astype(BF16)

    @pl.loop(0, steps)
    def _(step):
        here = pl.ds(pl.multiple_of(step * CHUNK, CHUNK), CHUNK)
        slope[here, :] = mm(latent_ref[here, :], w1_ref[:width, :])

    def project(rows, value):
        high = value.astype(BF16)
        proj[rows, :width] = high
        proj[rows, width:] = (value - high.astype(F32)).astype(BF16)

    table[:nodes, :] = node
    project(slice(slots, slots + nodes), mm(node, w1_ref[2 * width :, :]))
    wait_in()
    table[nodes:, :] = unpack(halo_in[...]).astype(BF16)
    project(slice(0, slots), mm(table[...], w1_ref[width : 2 * width, :]))

    @pl.loop(0, steps)
    def _(step):
        here = pl.ds(pl.multiple_of(step * CHUNK, CHUNK), CHUNK)
        picked = mm_rows(pick_t[:, here], proj[...])
        pre = slope[here, :] + (picked[:, :width] + picked[:, width:])
        hid, slope_here = silu_parts(pre)
        hidden[here, :] = hid
        slope[here, :] = slope_here
        hat_here, inv_here = normalize(mm(hid, w2_ref[...]))
        hat[here, :] = hat_here
        inv[here, :] = inv_here
        rows_bf[here, :] = (
            latent_ref[here, :].astype(F32) + hat_here * gain_ref[...]
        ).astype(BF16)

    aggregate = mm(pick_t[slots:, :], rows_bf[...]).astype(BF16)
    node_pre = mm(node, nw1_ref[:width, :]) + mm(aggregate, nw1_ref[width:, :])
    node_hidden, node_slope = silu_parts(node_pre)
    node_hat, node_inv = normalize(mm(node_hidden, nw2_ref[...]))
    node_dy = node_cot_ref[...].astype(F32)
    node_gain_part = jnp.sum(node_dy * node_hat, axis=0, keepdims=True) * node_scale
    node_mgrad = norm_back(node_dy, node_hat, node_inv, ngain_ref[...]).astype(BF16)
    grad_n2[...] = mm_rows(node_hidden, node_mgrad)
    node_agrad = (mm_cols(node_mgrad, nw2_ref[...]) * node_slope).astype(BF16)
    grad_n1[:width, :] = mm_rows(node, node_agrad)
    grad_n1[width : 2 * width, :] = mm_rows(aggregate, node_agrad)
    blank = jnp.zeros((16, width), F32)
    n1_rows, n2_rows = 2 * width // n, width // n
    fill(0, ((grad_n1, node_scale, n1_rows), (grad_n2, node_scale, n2_rows)), blank)
    agg_bf[...] = mm_cols(node_agrad, nw1_ref[width:, :]).astype(BF16)
    base_out[...] = node_dy + mm_cols(node_agrad, nw1_ref[:width, :])
    gain_sum[...] = jnp.zeros_like(gain_sum)

    def backward(first, last):
        @pl.loop(first, last)
        def _(step):
            here = pl.ds(pl.multiple_of(step * CHUNK, CHUNK), CHUNK)
            total = cot_ref[here, :].astype(F32) + mm_rows(pick_t[slots:, here], agg_bf[...])
            hat_here = hat[here, :]
            product = total * hat_here
            gain_sum[...] += jnp.sum(product.reshape(CHUNK // 8, 8, width), axis=0)
            mgrad = norm_back(total, hat_here, inv[here, :], gain_ref[...]).astype(BF16)
            rows_bf[here, :] = mgrad
            ag = (mm_cols(mgrad, w2_ref[...]) * slope[here, :]).astype(BF16)
            agrad[here, :] = ag
            edge_out[here, :] = (total + mm_cols(ag, w1_ref[:width, :])).astype(BF16)

    third = steps // 3
    backward(0, third)
    advance(0, 0)
    backward(third, steps)

    edge_gain_part = jnp.sum(gain_sum[...], axis=0, keepdims=True) * edge_scale
    row_id = lax.broadcasted_iota(jnp.int32, (32, width), 0)
    tail = jnp.where(row_id == 0, edge_gain_part, jnp.where(row_id == 1, node_gain_part, 0.0))
    grad_w2[...] = mm_rows(hidden[...], rows_bf[...])
    fill(1, ((grad_w2, edge_scale, width // n),), tail)
    if bits > 2:
        advance(0, 1)
    sums = mm(pick_t[...], agrad[...]).astype(BF16)
    by_slot, by_target = sums[:slots, :], sums[slots:, :]
    slot_sums = mm_cols(by_slot, w1_ref[width : 2 * width, :])
    slot_send[...] = pack(slot_sums[nodes:, :].reshape(n, halo // n, width))
    back, wait_back, wait_sent = swap_blocks(n, me, slot_send, slot_in, back_send, back_recv)
    grad_w1[:width, :] = mm_rows(latent_ref[...], agrad[...])
    grad_w1[width : 2 * width, :] = mm_rows(table[...], by_slot)
    grad_w1[2 * width :, :] = mm_rows(node, by_target)
    fill(2, ((grad_w1, edge_scale, 3 * width // n),), blank)
    back()
    base_out[...] += slot_sums[:nodes, :] + mm_cols(by_target, w1_ref[2 * width :, :])

    level = [2, 0, 0]
    if bits <= 2:
        level[0] = 1
    while min(level) < bits:
        for w in (1, 0, 2):
            if level[w] < bits:
                advance(w, level[w])
                level[w] += 1
    wait_back()
    slot_out[...] = slot_in[...]
    for copy in copies.values():
        copy.wait_send()
    wait_out()
    wait_sent()


def finish_kernel(
    rows_of,
    edge_ref,
    base_ref,
    slot_ref,
    index_ref,
    node_sum,
    w2_sum,
    w1_sum,
    edge_out,
    node_out,
    w1_out,
    w2_out,
    n1_out,
    n2_out,
    sem,
):
    copy = pltpu.make_async_copy(edge_ref, edge_out, sem)
    copy.start()
    r1, r2, r3, r4 = rows_of
    nodes, halo = base_ref.shape[0], slot_ref.shape[0] * slot_ref.shape[1] // 2
    skip = index_ref.shape[1] - halo
    owner = (
        lax.broadcasted_iota(jnp.int32, (nodes, halo), 0) == index_ref[:, skip:]
    ).astype(F32).astype(BF16)
    node_out[...] = (base_ref[...] + mm(owner, unpack(slot_ref[...]).astype(BF16))).astype(BF16)
    w1_out[...] = w1_sum[:r1, :]
    w2_out[...] = w2_sum[:r2, :]
    n1_out[...] = node_sum[:r3, :]
    n2_out[...] = node_sum[r3 : r3 + r4, :]
    copy.wait()


def round_up(rows):
    return -(-rows // 16) * 16


def local(
    n,
    node_latent,
    edge_latent,
    node_cotangent,
    edge_cotangent,
    sender_slot,
    receiver,
    send_index,
    edge_w1,
    edge_w2,
    edge_gain,
    node_w1,
    node_w2,
    node_gain,
):
    nodes, width = node_latent.shape
    edges = edge_latent.shape[0]
    cap = send_index.shape[2]
    half = width // 2
    bits = n.bit_length() - 1
    node_scale = 1.0 / math.sqrt(nodes * n)
    edge_scale = 1.0 / math.sqrt(edges * n)
    rows_of = tuple(w.shape[0] // n for w in (edge_w1, edge_w2, node_w1, node_w2))
    waves = (
        round_up(rows_of[2] + rows_of[3]),
        round_up(rows_of[1] + 2),
        round_up(rows_of[0]),
    )
    slots = nodes + n * cap
    vmem = pl.BlockSpec(memory_space=pltpu.VMEM)
    anywhere = pl.BlockSpec(memory_space=pl.ANY)
    packed = jax.ShapeDtypeStruct((n, 2 * cap, half), BF16)
    indices = jnp.concatenate([sender_slot, receiver, send_index.reshape(n * cap)]).reshape(1, -1)
    stacks = [pltpu.VMEM((n, block, half), BF16) for block in waves for _ in range(2)]
    landing = [
        pltpu.VMEM((n >> (level + 1), block, half), BF16)
        for block in waves
        for _ in range(2)
        for level in range(bits)
    ]

    edge_grad, base, slot_back, node_sum, w2_sum, w1_sum = pl.pallas_call(
        functools.partial(layer_kernel, n, waves, node_scale, edge_scale),
        out_shape=(
            jax.ShapeDtypeStruct((edges, width), BF16),
            jax.ShapeDtypeStruct((nodes, width), F32),
            packed,
        )
        + tuple(jax.ShapeDtypeStruct((block, width), F32) for block in waves),
        in_specs=[vmem] * 11,
        out_specs=(vmem,) * 6,
        scratch_shapes=[pltpu.VMEM(packed.shape, BF16)] * 4
        + [
            pltpu.VMEM((slots, width), BF16),
            pltpu.VMEM((slots + nodes, 2 * width), BF16),
            pltpu.VMEM((slots + nodes, edges), BF16),
            pltpu.VMEM((edges, width), F32),
            pltpu.VMEM((edges, width), BF16),
            pltpu.VMEM((edges, width), F32),
            pltpu.VMEM((edges, 1), F32),
            pltpu.VMEM((edges, width), BF16),
            pltpu.VMEM((edges, width), BF16),
            pltpu.VMEM((nodes, width), BF16),
            pltpu.VMEM((8, width), F32),
            pltpu.VMEM((3 * width, width), F32),
            pltpu.VMEM((width, width), F32),
        ]
        + [pltpu.SemaphoreType.DMA((n,))] * 4
        + [pltpu.SemaphoreType.DMA((3, 2, bits))] * 2
        + stacks
        + landing,
        compiler_params=pltpu.CompilerParams(
            collective_id=0, has_side_effects=True, vmem_limit_bytes=VMEM_LIMIT
        ),
    )(
        indices,
        node_latent,
        edge_latent,
        node_cotangent,
        edge_cotangent,
        edge_w1,
        edge_w2,
        edge_gain.reshape(1, width),
        node_w1,
        node_w2,
        node_gain.reshape(1, width),
    )

    edge_grad, node_grad, w1_grad, w2_grad, n1_grad, n2_grad = pl.pallas_call(
        functools.partial(finish_kernel, rows_of),
        out_shape=(
            jax.ShapeDtypeStruct((edges, width), BF16),
            jax.ShapeDtypeStruct((nodes, width), BF16),
        )
        + tuple(jax.ShapeDtypeStruct((rows, width), F32) for rows in rows_of),
        in_specs=[anywhere] + [vmem] * 6,
        out_specs=(anywhere,) + (vmem,) * 5,
        scratch_shapes=[pltpu.SemaphoreType.DMA],
        compiler_params=pltpu.CompilerParams(vmem_limit_bytes=VMEM_LIMIT),
    )(edge_grad, base, slot_back, indices, node_sum, w2_sum, w1_sum)
    share = width // n
    at = lax.axis_index("node") * share
    gains = lax.dynamic_slice(w2_sum, (rows_of[1], at), (2, share))
    return node_grad, edge_grad, w1_grad, w2_grad, gains[0], n1_grad, n2_grad, gains[1]


def solution(mesh):
    rows = P(("groups", "node"), None)
    flat = P(("groups", "node"))
    return jax.shard_map(
        functools.partial(local, mesh.shape["node"]),
        mesh=mesh,
        in_specs=(rows, rows, rows, rows, flat, flat, P(("groups", "node"), None, None))
        + (P(),) * 6,
        out_specs=(rows, rows, rows, rows, flat, rows, rows, flat),
        check_vma=False,
    )
```

time: 96.7 us -> 116 us (1.20)
  Pallas kernels: 78.2 us -> 111 us
  local copies, waits for them, and re-layouts: 17.4 us -> 2.73 us
    pallas_call x3 -> x2, Pallas kernels: 78.2 us -> 111 us  [the longest x1 60.4 us: local(): pl.pallas_call(functools.partial(layer_kernel, n, waves, node_scale, edge...]
    unnamed x6 -> x1, local copies, waits for them, and re-layouts: 8.5 us -> 0.76 us
    reshape x6 -> x2, local copies, waits for them, and re-layouts: 7.61 us -> 0.69 us  [the longest x1 0.6 us: local(): jnp.concatenate([sender_slot, receiver, send_index.reshape(n * cap)])]
where the time goes in v2:
time: 116 us; the launch traced here: 115 us
  Pallas kernels  111 us (96%)
  local copies, waits for them, and re-layouts  2.73 us (2%)
    pallas_call x1, Pallas kernels, local(): pl.pallas_call(functools.partial(layer_kernel, n, waves, node_scale, edge...  60.4 us
    pallas_call x1, Pallas kernels, local(): pl.pallas_call(functools.partial(finish_kernel, rows_of), out_shape=(jax....  50.8 us

profile of v2, /device:TPU:0, one launch (start us, length us, event | category | flops | bytes accessed | tf_op | source)
XLA Modules:
  0.0 115.3 jit_solution(8458445037503716596)
XLA Ops:
  0.6 0.8 copy.22
  1.4 0.1 reshape.28
  1.5 0.7 pad_add_fusion
  2.2 0.6 reshape.29.index_ref
  2.8 60.4 %shard_map.188 = (bf16[1536,512]{1,0:T(8,128)(2,1)}, f32[192,512]{1,0:T(8,128)}, bf16[16,16,256]{2,1,0:T(8,128)(2,1)}, f32[96,512]{1,0:T(8,128)}, f32[48,512]{1,0:T(8,128)}, /*index=5*/f32[96,512]{1,0:T(8,128)}) custom-call(s32[1,3200]{1,0:T(1,128)} %reshape.29.index_ref, bf16[192,512]{1,0:T(8,128)(2,1)} %node_ref.1, bf16[1536,512]{1,0:T(8,128)(2,1)} %latent_ref.1, ...), custom_call_target="tpu_custom_call" | custom-call | tf_op jit(solution)/shard_map/pallas_call | solution.py:444
  63.2 50.8 %shard_map.189 = (bf16[1536,512]{1,0:T(8,128)(2,1)}, bf16[192,512]{1,0:T(8,128)(2,1)}, f32[96,512]{1,0:T(8,128)}, f32[32,512]{1,0:T(8,128)}, f32[64,512]{1,0:T(8,128)}, /*index=5*/f32[32,512]{1,0:T(8,128)}) custom-call(bf16[1536,512]{1,0:T(8,128)(2,1)} %get-tuple-element.20.edge_ref, f32[192,512]{1,0:T(8,128)} %get-tuple-element.21.base_ref, ...), custom_call_target="tpu_custom_call" | custom-call | tf_op jit(solution)/shard_map/pallas_call | solution.py:491
  114.0 0.8 constant_dynamic-slice_fusion
  114.8 0.5 slice_bitcast_fusion

commit v3 on v2

--- a/solution.py
+++ b/solution.py
@@ -495,7 +495,7 @@
             jax.ShapeDtypeStruct((nodes, width), BF16),
         )
         + tuple(jax.ShapeDtypeStruct((rows, width), F32) for rows in rows_of),
-        in_specs=[anywhere] + [vmem] * 6,
+        in_specs=[vmem] * 7,
         out_specs=(anywhere,) + (vmem,) * 5,
         scratch_shapes=[pltpu.SemaphoreType.DMA],
         compiler_params=pltpu.CompilerParams(vmem_limit_bytes=VMEM_LIMIT),

time: 116 us -> 68.5 us (0.59)
  Pallas kernels: 111 us -> 64 us
    pallas_call x1, Pallas kernels: 50.8 us -> 3.66 us  [local(): pl.pallas_call(functools.partial(finish_kernel, rows_of), out_shape=(jax....]
where the time goes in v3:
time: 68.5 us; the launch traced here: 68.1 us
  Pallas kernels  64 us (93%)
  local copies, waits for them, and re-layouts  2.73 us (4%)
  other arithmetic  0.73 us (1%)
    pallas_call x1, Pallas kernels, local(): pl.pallas_call(functools.partial(layer_kernel, n, waves, node_scale, edge...  60.4 us
    pallas_call x1, Pallas kernels, local(): pl.pallas_call(functools.partial(finish_kernel, rows_of), out_shape=(jax....  3.66 us

profile of v3, /device:TPU:0, one launch (start us, length us, event | category | flops | bytes accessed | tf_op | source)
XLA Modules:
  0.0 68.1 jit_solution(11636651616495938573)
XLA Ops:
  0.6 0.8 %copy.22 = s32[1,16,8]{2,1,0:T(8,128)S(1)} copy(s32[1,16,8]{1,2,0:T(8,128)} %param.19) | data formatting | bytes 1024 | tf_op args[6]
  1.4 0.1 reshape.28
  1.5 0.7 %pad_add_fusion = s32[3200]{0:T(1024)S(1)} fusion(s32[128]{0:T(128)S(1)} %reshape.28, s32[1536]{0:T(1024)} %param.18, s32[1536]{0:T(1024)} %param.17), kind=kLoop, calls=%fused_computation | loop fusion | flops 6400 | bytes 25600 | tf_op jit(solution)/shard_map/concatenate | solution.py:435
  2.2 0.6 reshape.29.index_ref
  2.8 60.4 %shard_map.188 = (bf16[1536,512]{1,0:T(8,128)(2,1)}, f32[192,512]{1,0:T(8,128)}, bf16[16,16,256]{2,1,0:T(8,128)(2,1)}, f32[96,512]{1,0:T(8,128)}, f32[48,512]{1,0:T(8,128)}, /*index=5*/f32[96,512]{1,0:T(8,128)}) custom-call(s32[1,3200]{1,0:T(1,128)} %reshape.29.index_ref, bf16[192,512]{1,0:T(8,128)(2,1)} %node_ref.1, bf16[1536,512]{1,0:T(8,128)(2,1)} %latent_ref.1, ...), custom_call_target="tpu_custom_call" | custom-call | tf_op jit(solution)/shard_map/pallas_call | solution.py:444
  63.2 3.7 %shard_map.189 = (bf16[1536,512]{1,0:T(8,128)(2,1)}, bf16[192,512]{1,0:T(8,128)(2,1)}, f32[96,512]{1,0:T(8,128)}, f32[32,512]{1,0:T(8,128)}, f32[64,512]{1,0:T(8,128)}, /*index=5*/f32[32,512]{1,0:T(8,128)}) custom-call(bf16[1536,512]{1,0:T(8,128)(2,1)} %get-tuple-element.20.edge_ref, f32[192,512]{1,0:T(8,128)} %get-tuple-element.21.base_ref, ...), custom_call_target="tpu_custom_call" | custom-call | tf_op jit(solution)/shard_map/pallas_call | solution.py:491
  66.9 0.8 %constant_dynamic-slice_fusion = f32[2,32]{1,0:T(2,128)S(1)} fusion(f32[48,512]{1,0:T(8,128)} %get-tuple-element.24.w2_sum, s32[]{:T(128)S(6)} %select_n.3), kind=kLoop, calls=%fused_computation.3 | loop fusion | bytes 516 | tf_op jit(solution)/shard_map/dynamic_slice | solution.py:505
  67.6 0.5 slice_bitcast_fusion
